TPU v7x, 32 devices: a whole 2x2x4 slice. The times are simulated.
32 devices in a mesh: ens: 4 (over y, x), grid: 8 (over z, core).
Axes of the slice: x: 2, y: 2, z: 4, core: 2. Of those that a mesh axis runs over, the one named last changes fastest.
Arguments:
- latent: bfloat16 [4, 1024, 2048], P('ens', None, 'grid'), may hold values from -24 to 24
- w_in: bfloat16 [1024, 1024], replicated, may hold values from -0.1875 to 0.1875
- w_out: bfloat16 [99, 1024], replicated, may hold values from -0.1875 to 0.1875
- target: float32 [99, 2048], P(None, 'grid'), may hold values from -6 to 6
- area: float32 [2048], P('grid'), may hold values from 0.05 to 3, as said below
- var_weight: float32 [99], replicated, may hold values from 0.2 to 2
Outputs:
- loss: float32 [], replicated
- grad_latent: bfloat16 [4, 1024, 2048], P('ens', None, 'grid')
- grad_in: float32 [1024, 1024], P('ens', 'grid')
- grad_out: float32 [99, 1024], P(None, 'grid')
Inputs may be any that keep to these rules, and one draw needn't show every extreme that they name: Every area weight is positive.
All inputs are finite; a program needn't handle non-finite values.
Results may differ from a plain program's by a relative error of at most 0.013.
Values may be sent and summed in bfloat16 or wider, within the bound.
A program may use at most 64 MiB of HBM per device.

v0:
```python
import jax
import jax.numpy as jnp
from jax import lax
from jax.sharding import PartitionSpec as P

VARS = 99


smooth_sq = 0.01
gelu_c = 0.7978845608
gelu_k = 0.044715


def gelu_value(value):
    inner = jnp.tanh(gelu_c * (value + gelu_k * value * value * value))
    return 0.5 * value * (1.0 + inner)


def gelu_slope(value):
    inner = jnp.tanh(gelu_c * (value + gelu_k * value * value * value))
    return 0.5 * (1.0 + inner) + 0.5 * value * (1.0 - inner * inner) * gelu_c * (
        1.0 + 3.0 * gelu_k * value * value
    )


def distance(value):
    return jnp.sqrt(value * value + smooth_sq)


def distance_slope(value):
    return value / jnp.sqrt(value * value + smooth_sq)


def per_device(latent, w_in, w_out, target, area, var_weight):
    count = float(lax.axis_size("ens"))
    points_all = lax.axis_size("grid") * area.shape[0]
    features = latent[0]
    preact = jnp.dot(w_in, features, preferred_element_type=jnp.float32)
    hidden = gelu_value(preact).astype(jnp.bfloat16)
    decoded = jnp.dot(w_out, hidden, preferred_element_type=jnp.float32)
    weight_total = lax.psum(jnp.sum(area), "grid")
    spread = decoded[None] - lax.all_gather(decoded[None], "ens", axis=0, tiled=True)
    pair_sum = jnp.sum(distance(spread), 0)
    pair_slope = jnp.sum(distance_slope(spread), 0)
    weight = area[None, :] * var_weight[:, None]
    local = distance(decoded - target) / count - pair_sum / (2.0 * count * (count - 1.0))
    loss = lax.psum(jnp.sum(weight * local), ("ens", "grid")) / (weight_total * VARS)
    factor = points_all / (weight_total * VARS)
    dout = (
        factor
        * weight
        * (distance_slope(decoded - target) / count - pair_slope / (count * (count - 1.0)))
    ).astype(jnp.bfloat16)
    dhidden = lax.dot_general(
        w_out, dout, (((0,), (0,)), ((), ())), preferred_element_type=jnp.float32
    )
    dpre = (dhidden * gelu_slope(preact)).astype(jnp.bfloat16)
    grad_lat = lax.dot_general(
        w_in, dpre, (((0,), (0,)), ((), ())), preferred_element_type=jnp.float32
    ).astype(jnp.bfloat16)
    term_in = lax.dot_general(
        dpre, features, (((1,), (1,)), ((), ())), preferred_element_type=jnp.float32
    )
    term_out = lax.dot_general(
        dout, hidden, (((1,), (1,)), ((), ())), preferred_element_type=jnp.float32
    )
    part_in = lax.psum_scatter(
        term_in.astype(jnp.bfloat16), "grid", scatter_dimension=1, tiled=True
    ).astype(jnp.float32)
    total_in = lax.psum_scatter(part_in, "ens", scatter_dimension=0, tiled=True)
    part_out = lax.psum_scatter(
        term_out.astype(jnp.bfloat16), "grid", scatter_dimension=1, tiled=True
    ).astype(jnp.float32)
    total_out = lax.psum(part_out, "ens")
    ratio = 1.0 / jnp.sqrt(jnp.float32(points_all) * jnp.float32(count))
    return (loss, grad_lat[None], ratio * total_in, ratio * total_out)


def solution(mesh):
    in_specs = (P("ens", None, "grid"), P(), P(), P(None, "grid"), P("grid"), P())
    out_specs = (P(), P("ens", None, "grid"), P("ens", "grid"), P(None, "grid"))
    return jax.shard_map(
        per_device, mesh=mesh, in_specs=in_specs, out_specs=out_specs, check_vma=False
    )
```

profile of v0, /device:TPU:0, one launch (start us, length us, event | category | flops | bytes accessed | tf_op | source)
XLA Modules:
  0.0 153.4 jit_solution(2709586363687377695)
XLA Ops:
  7.2 0.0 copy-start
  7.2 0.0 reduce-scatter.10.cloned.1.call-start
  7.2 1.4 reduce_sum.38
  8.7 18.7 %psum.22 = f32[]{:T(128)} all-reduce(f32[]{:T(128)} %reduce_sum.38), channel_id=1, replica_groups=mesh['ens'=4,'grid'=8] {'grid'}, use_global_device_ids=true, to_apply=%region_4.0 | all-reduce | flops 1 | bytes 8 | tf_op jit(solution)/shard_map/psum | solution.py:41
  27.3 0.0 copy-done
  27.3 0.0 copy-start.2
  27.3 2.9 %multiply_convert_fusion = (bf16[1024,256]{1,0:T(8,128)(2,1)S(1)}, f32[1024,256]{1,0:T(8,128)}) fusion(bf16[1024,1024]{1,0:T(8,128)(2,1)S(1)} %copy-done, bf16[1,1024,256]{2,1,0:T(8,128)(2,1)} %param.6), kind=kOutput, calls=%fused_computation.14 | convolution fusion | flops 539230208 | bytes 4194304 | tf_op jit(solution)/shard_map/dot_general | solution.py:38
  30.2 0.0 copy-start.3
  30.2 0.0 copy-start.4
  30.3 0.0 copy-start.5
  30.3 0.0 copy-done.2
  30.3 0.2 fusion.15
  30.5 9.7 %all-gather.1 = f32[4,99,256]{2,1,0:T(8,128)S(1)} all-gather(f32[1,99,256]{2,1,0:T(8,128)S(1)} %bitcast.37), channel_id=2, replica_groups=mesh['ens'=4,'grid'=8] {'ens'}, dimensions={0}, use_global_device_ids=true | all-gather | bytes 506880 | tf_op jit(solution)/shard_map/all_gather | solution.py:42
  40.8 0.2 divide_reduce_fusion
  41.1 0.0 copy-done.3
  41.1 0.0 copy-done.4
  41.1 0.0 copy-done.5
  41.1 0.7 fusion.14
  41.8 0.0 copy-start.1
  41.8 2.2 %fusion.1 = bf16[1024,256]{1,0:T(8,128)(2,1)S(1)} fusion(bf16[99,256]{1,0:T(8,128)(2,1)S(1)} %get-tuple-element.14, bf16[99,1024]{1,0:T(8,128)(2,1)} %param.8, f32[1024,256]{1,0:T(8,128)} %get-tuple-element.17), kind=kOutput, calls=%fused_computation.5 | convolution fusion | flops 56885248 | bytes 1826304 | tf_op jit(solution)/shard_map/dot_general | solution.py:54
  44.0 0.0 copy-done.1
  44.0 2.0 %convolution_convert_fusion = bf16[1024,1024]{1,0:T(8,128)(2,1)} fusion(bf16[1024,256]{1,0:T(8,128)(2,1)S(1)} %fusion.1, bf16[1,1024,256]{2,1,0:T(8,128)(2,1)S(1)} %copy-done.1), kind=kOutput, calls=%fused_computation | convolution fusion | flops 537919488 | bytes 3145728 | tf_op jit(solution)/shard_map/dot_general | solution.py:61
  46.1 4.0 %copy.15 = bf16[1024,1024]{0,1:T(8,128)(2,1)} copy(bf16[1024,1024]{1,0:T(8,128)(2,1)} %convolution_convert_fusion) | data formatting | bytes 4194304
  50.0 0.0 reduce-scatter.10.cloned.1.call-update
  50.1 0.0 reduce-scatter.12.cloned.1.call-start
  50.1 0.3 convolution_convert_fusion.2
  50.4 0.9 copy.17
  51.3 0.0 reduce-scatter.12.cloned.1.call-update
  51.3 0.0 reduce-scatter.8.cloned.1.call-start
  51.4 31.9 %reduce-scatter.10.cloned.1.call-done = bf16[128,1024]{1,0:T(8,128)(2,1)} async-done(((bf16[1024,1024]{1,0:T(8,128)(2,1)}), bf16[128,1024]{1,0:T(8,128)(2,1)}) %reduce-scatter.10.cloned.1.call-update) | async-done | bytes 262160
  83.3 1.1 copy.16
  84.4 0.8 convert_element_type.33
  85.2 0.0 reduce-scatter.8.cloned.1.call-update
  85.2 38.1 %psum.21 = f32[]{:T(128)} all-reduce(f32[]{:T(128)} %get-tuple-element.15), channel_id=1, replica_groups=mesh['ens'=4,'grid'=8] {'ens','grid'}, use_global_device_ids=true, to_apply=%region_2.0 | all-reduce | flops 1 | bytes 8 | tf_op jit(solution)/shard_map/psum | solution.py:47
  124.0 0.7 fusion.2
  124.7 1.0 copy.13
  125.7 0.0 reduce-scatter.12.cloned.1.call-done
  125.7 0.9 copy.18
  126.6 16.9 %psum.23 = f32[99,128]{1,0:T(8,128)S(1)} all-reduce(bf16[99,128]{1,0:T(8,128)(2,1)S(1)} %copy.18), channel_id=1, replica_groups=mesh['ens'=4,'grid'=8] {'ens'}, use_global_device_ids=true, to_apply=%region_9.0 | all-reduce | flops 12672 | bytes 76032 | tf_op jit(solution)/shard_map/psum | solution.py:74
  143.5 0.6 broadcast_multiply_fusion.1
  144.1 0.0 reduce-scatter.8.cloned.1.call-done
  144.1 1.6 %broadcast_multiply_fusion = f32[256,128]{1,0:T(8,128)} fusion(f32[256,128]{1,0:T(8,128)} %reduce-scatter.8.cloned.1.call-done), kind=kLoop, calls=%fused_computation.27 | loop fusion | flops 32768 | bytes 262144 | tf_op jit(solution)/shard_map/mul | solution.py:76
Async XLA Ops:
  7.2 20.2 %copy-start = (bf16[1024,1024]{1,0:T(8,128)(2,1)S(1)}, bf16[1024,1024]{1,0:T(8,128)(2,1)}, u32[]{:S(2)}) copy-start(bf16[1024,1024]{1,0:T(8,128)(2,1)} %param.7) | copy-start | bytes 6291460
  7.2 76.1 %reduce-scatter.10.cloned.1.call-start = ((), (), s32[]{:S(2)}) async-start(), calls=%async_computation.4 | async-start | bytes 2359296
  27.3 2.9 %copy-start.2 = (bf16[99,1024]{1,0:T(8,128)(2,1)S(1)}, bf16[99,1024]{1,0:T(8,128)(2,1)}, u32[]{:S(2)}) copy-start(bf16[99,1024]{1,0:T(8,128)(2,1)} %param.8) | copy-start | bytes 608260
  30.2 10.8 %copy-start.3 = (f32[99,256]{1,0:T(8,128)S(1)}, f32[99,256]{1,0:T(8,128)}, u32[]{:S(2)}) copy-start(f32[99,256]{1,0:T(8,128)} %param.9) | copy-start | bytes 304132
  30.2 10.8 %copy-start.4 = (f32[256]{0:T(256)S(1)}, f32[256]{0:T(256)}, u32[]{:S(2)}) copy-start(f32[256]{0:T(256)} %param.10) | copy-start | bytes 3076
  30.3 10.9 %copy-start.5 = (f32[99]{0:T(128)S(1)}, f32[99]{0:T(128)}, u32[]{:S(2)}) copy-start(f32[99]{0:T(128)} %param.11) | copy-start | bytes 1192
  41.8 2.2 %copy-start.1 = (bf16[1,1024,256]{2,1,0:T(8,128)(2,1)S(1)}, bf16[1,1024,256]{2,1,0:T(8,128)(2,1)}, u32[]{:S(2)}) copy-start(bf16[1,1024,256]{2,1,0:T(8,128)(2,1)} %param.6) | copy-start | bytes 1572868
  50.1 75.7 %reduce-scatter.12.cloned.1.call-start = ((), (), s32[]{:S(2)}) async-start(), calls=%async_computation.5 | async-start | bytes 294912
  51.3 92.8 %reduce-scatter.8.cloned.1.call-start = ((), (), s32[]{:S(2)}) async-start(), calls=%async_computation.3 | async-start | bytes 655360 | tf_op jit(solution)/shard_map/reduce_scatter | solution.py:70
Sparse Core Ops, SparseCore 0:
  50.2 33.0 reduce-scatter.9
  85.5 29.1 reduce-scatter.11
  117.8 23.0 reduce-scatter.7
where the time goes:
time: 154 us; the launch traced here: 153 us
  blocking collectives  83.3 us (54%)
  waiting for transfers between devices  31.9 us (21%)
  between operations  16.3 us (11%)
  matrix products  8.39 us (5%)
  local copies, waits for them, and re-layouts  7.84 us (5%)
  other arithmetic  5.41 us (4%)
    psum x1, blocking collectives, per_device(): lax.psum(jnp.sum(weight * local), ('ens', 'grid')) / (weight_total * VARS)  38.1 us
    unnamed x5, waiting for transfers between devices  31.9 us
    psum x1, blocking collectives, per_device(): weight_total = lax.psum(jnp.sum(area), 'grid')  18.7 us
    psum x1, blocking collectives, per_device(): total_out = lax.psum(part_out, 'ens')  16.9 us
    all_gather x1, blocking collectives, per_device(): lax.all_gather(decoded[None], 'ens', axis=0, tiled=True)  9.66 us
    unnamed x17, local copies, waits for them, and re-layouts  7.84 us
  transfers between devices with their start and end apart: 3, of which 1 were waited for; matrix products, arithmetic and copies ran while one was open for 4% of the time, Pallas kernels for 0%

commit v1 on v0

v1 whole, which is shorter than its diff:
```python
import functools

import jax
import jax.numpy as jnp
import numpy as np
from jax import lax
from jax.experimental import pallas as pl
from jax.experimental.pallas import tpu as pltpu
from jax.sharding import PartitionSpec as P

SMOOTH = 0.01
GELU_C = 0.7978845608
GELU_K = 0.044715
F32 = jnp.float32
BF16 = jnp.bfloat16


def dot_nn(a, b):
    return jnp.dot(a, b, preferred_element_type=F32)


def dot_nt(a, b):
    return lax.dot_general(a, b, (((1,), (1,)), ((), ())), preferred_element_type=F32)


def dot_tn(a, b):
    return lax.dot_general(a, b, (((0,), (0,)), ((), ())), preferred_element_type=F32)


class Sizes:
    def __init__(self, n, ng, hid, lat, nvars, pts):
        self.n, self.ng, self.hid, self.lat, self.nvars, self.pts = n, ng, hid, lat, nvars, pts
        self.nz = ng // 2
        self.nb = n.bit_length() - 1
        self.cols = lat // ng
        self.rows_e = hid // n
        self.half = self.rows_e // 2
        self.vrow = -(-(-(-nvars // n)) // 16) * 16
        self.vpad = self.vrow * n
        self.tile = max(256, 2 * self.cols)
        self.tiles = hid // self.tile
        self.copies = 3 * ng + 4 * n + 8 + self.tiles + (2 * self.nz + 1) * (self.nb + 1) + 2 * self.nz + n


def stage_index(nb, order, stage, value):
    index = [slice(None)] * nb
    for bit in order[:stage]:
        index[nb - 1 - bit] = 0
    index[nb - 1 - order[stage]] = value
    return tuple(index)


def kernel(
    s,
    lat_hbm, win_hbm, wout_ref, target_ref, area_ref, vw_ref,
    loss_ref, glat_hbm, gin_ref, gout_ref,
    lat_s, latp, win_s, wo32, wo_s, wot, hid_s, hidp, slope_s, dec_s, dec_in, tgt_s, vrow_s, vcol_s, area_all,
    dout_o, dout_s, doutp, loss_e, loss_g, dpre_s, dprep, glat_s, gall,
    acc, snd, acc_o, snd_o, tmp_o, zsnd, zrcv, zsnd_o, zrcv_o, *rest,
):
    nb, n, ng, nz = s.nb, s.n, s.ng, s.nz
    rcv, rcv_o = rest[:nb], rest[nb:2 * nb]
    send_sem, recv_sem, local_sem = rest[2 * nb:]
    me = lax.axis_index("ens")
    g = lax.axis_index("grid")
    core = g % 2
    chip = g // 2
    bits = [(me // (1 << i)) % 2 for i in range(nb)]
    used = [0]

    def ens_peer(r):
        return sum((bits[i] + ((r >> i) & 1) * (1 - 2 * bits[i])) * (1 << i) for i in range(nb))

    def remote(src, dst, device):
        i = used[0]
        used[0] += 1
        copy = pltpu.make_async_remote_copy(
            src_ref=src, dst_ref=dst, send_sem=send_sem.at[i], recv_sem=recv_sem.at[i],
            device_id=device, device_id_type=pl.DeviceIdType.MESH,
        )
        copy.start()
        sent.append(copy)
        return copy

    sent = []
    twin = {"grid": g + 1 - 2 * core}
    ens_peers = [None] + [{"ens": ens_peer(r)} for r in range(1, n)]
    grid_peers = [None] + [{"grid": (g + o) % ng} for o in range(1, ng)]

    get_lat = pltpu.make_async_copy(lat_hbm, lat_s, local_sem.at[0])
    get_win = pltpu.make_async_copy(win_hbm, win_s, local_sem.at[1])
    get_lat.start()
    get_win.start()
    barrier = pltpu.get_barrier_semaphore()
    for peer in ens_peers[1:] + grid_peers[1:]:
        pl.semaphore_signal(barrier, inc=1, device_id=peer, device_id_type=pl.DeviceIdType.MESH)

    arow = area_ref[...].reshape(1, s.pts)
    area_all[0] = jnp.broadcast_to(arow, (8, s.pts))
    wo32[...] = jnp.zeros_like(wo32)
    wo32[0:s.nvars, :] = wout_ref[...].astype(F32)
    wo_s[...] = wo32[...].astype(BF16)
    tgt_s[...] = jnp.zeros_like(tgt_s)
    tgt_s[0:s.nvars, :] = target_ref[...]
    vrow_s[...] = jnp.zeros_like(vrow_s)
    vrow_s[0:1, 0:s.nvars] = vw_ref[...].reshape(1, s.nvars)

    pl.semaphore_wait(barrier, n + ng - 2)
    lat_copy = remote(lat_hbm.at[:, 1 - core], latp, twin)
    area_copies = [remote(area_all.at[0], area_all.at[o], grid_peers[o]) for o in range(1, ng)]

    get_lat.wait()
    get_win.wait()
    span = s.tile // (2 * s.cols)

    def forward(i, carry):
        rows = pl.ds(pl.multiple_of(i * s.tile, s.tile), s.tile)
        v = dot_nn(win_s[rows, :], lat_s[...].reshape(s.lat, s.pts))
        t = jnp.tanh(GELU_C * (v + GELU_K * v * v * v))
        hid_s[pl.ds(i * span, span)] = (0.5 * v * (1.0 + t)).astype(BF16).reshape(span, 2, s.cols, s.pts)
        slope_s[rows, :] = 0.5 * (1.0 + t) + 0.5 * v * (1.0 - t * t) * GELU_C * (1.0 + 3.0 * GELU_K * v * v)
        return carry

    lax.fori_loop(0, s.tiles, forward, 0)
    dec_s[...] = dot_nn(wo_s[...], hid_s[...].reshape(s.hid, s.pts)).reshape(n, s.vrow, s.pts)

    dec_copies = [remote(dec_s.at[ens_peer(r)], dec_in.at[r], ens_peers[r]) for r in range(1, n)]
    hid_copy = remote(hid_s.at[:, 1 - core], hidp, twin)
    dec_in[0] = dec_s[me]
    wot[...] = wo32[...].T.astype(BF16)
    square = (s.vpad, s.vpad)
    eye = lax.broadcasted_iota(jnp.int32, square, 0) == lax.broadcasted_iota(jnp.int32, square, 1)
    column = jnp.sum(jnp.where(eye, jnp.broadcast_to(vrow_s[0:1, :], square), 0.0), axis=1, keepdims=True)
    vcol_s[...] = jnp.broadcast_to(column, vcol_s.shape)
    mine = pl.ds(pl.multiple_of(me * s.vrow, s.vrow), s.vrow)
    weight = vcol_s[mine, 0:1] * arow
    target = tgt_s[mine, :]
    for copy in area_copies:
        copy.wait_recv()
    total = jnp.sum(area_all[...][:, 0, :].reshape(ng, s.pts), axis=1, keepdims=True)
    total = jnp.sum(total, axis=0, keepdims=True)
    scale = 1.0 / (total * float(s.nvars))
    wide = (float(ng * s.pts) * scale) * weight
    for copy in dec_copies:
        copy.wait_recv()
    members = [dec_in[r] for r in range(n)]
    slopes = [None] * n
    pairs = jnp.full((s.vrow, s.pts), float(n) * float(np.sqrt(np.float32(SMOOTH))), F32)
    for m in range(n):
        for k in range(m):
            u = members[m] - members[k]
            q = u * u + SMOOTH
            root = lax.rsqrt(q)
            pairs = pairs + 2.0 * (q * root)
            slope = u * root
            slopes[m] = slope if slopes[m] is None else slopes[m] + slope
            slopes[k] = -slope if slopes[k] is None else slopes[k] - slope
    local = pairs * (-1.0 / (2.0 * n * (n - 1.0)))
    dout_copies = []
    for r in range(n - 1, -1, -1):
        u = members[r] - target
        q = u * u + SMOOTH
        root = lax.rsqrt(q)
        local = local + (q * root) * (1.0 / n)
        d = (wide * (u * root * (1.0 / n) - slopes[r] * (1.0 / (n * (n - 1.0))))).astype(BF16)
        if r:
            dout_o[r] = d
            dout_copies.append(remote(dout_o.at[r], dout_s.at[me], ens_peers[r]))
        else:
            dout_s[me] = d
    part = jnp.sum(jnp.sum(weight * local, axis=1, keepdims=True), axis=0, keepdims=True)
    loss_e[0] = jnp.broadcast_to(part, (8, 128))
    loss_copies = [remote(loss_e.at[0], loss_e.at[r], ens_peers[r]) for r in range(1, n)]

    for copy in dout_copies:
        copy.wait_recv()
    dout_copy = remote(dout_s, doutp, twin)
    dout = dout_s[...].reshape(s.vpad, s.pts)
    dpre_copies = []
    for i in range(s.tiles):
        rows = pl.ds(i * s.tile, s.tile)
        dpre_s[rows, :] = (dot_nn(wot[rows, :], dout) * slope_s[rows, :]).astype(BF16)
        dpre_copies.append(remote(dpre_s.at[rows], dprep.at[rows], twin))

    def chip_at(k):
        return (chip + nz - 1 - k) % nz

    up, down = list(range(nb)), list(range(nb))[::-1]

    def relative(r):
        return tuple((r >> (nb - 1 - axis)) & 1 for axis in range(nb))

    def start(sums, send, into, order, stage):
        index = stage_index(nb, order, stage, 1)
        send[index] = sums[index].astype(BF16)
        bit = order[stage]
        return remote(send.at[index], into, ens_peers[1 << bit])

    def absorb(copy, sums, into, order, stage):
        copy.wait_recv()
        index = stage_index(nb, order, stage, 0)
        sums[index] = sums[index] + into[...].astype(F32)

    for copy in loss_copies:
        copy.wait_recv()
    here = loss_e[0]
    for r in range(1, n):
        here = here + loss_e[r]
    loss_g[0] = here
    loss_copies = [remote(loss_g.at[0], loss_g.at[o], grid_peers[o]) for o in range(1, ng)]

    hid_copy.wait_recv()
    dout_copy.wait_recv()
    for k in range(nz):
        z = chip_at(k)
        term = dot_nt(dout, hid_s[z, core]) + dot_nt(doutp[...].reshape(s.vpad, s.pts), hidp[z])
        tmp_o[...] = term.reshape(n, s.vrow, s.cols)
        for r in range(n):
            acc_o[relative(r) + (k,)] = tmp_o[ens_peer(r)]
    out_copy = start(acc_o, snd_o, rcv_o[0], up, 0)

    lat_copy.wait_recv()
    for copy in dpre_copies:
        copy.wait_recv()
    moves = []
    for k in range(nz):
        z = chip_at(k)
        own, other = lat_s[z, core], latp[z]
        for r in range(n):
            rows = pl.ds(pl.multiple_of(ens_peer(r) * s.rows_e, s.rows_e), s.rows_e)
            term = dot_nt(dpre_s[rows, :], own) + dot_nt(dprep[rows, :], other)
            acc[(k, 0) + relative(r)] = term[:s.half]
            acc[(k, 1) + relative(r)] = term[s.half:]
        moves.append([
            start(acc.at[k, h], snd.at[k, h], rcv[0].at[k, h], order, 0)
            for h, order in enumerate((up, down))
        ])

    width = s.lat // 4
    puts = []

    def latent_part(j):
        at = pl.ds(j * width, width)
        glat_s[at, :] = dot_tn(win_s[:, at], dpre_s[...]).astype(BF16)
        put = pltpu.make_async_copy(glat_s.at[at], glat_hbm.at[0, at], local_sem.at[2 + j])
        put.start()
        puts.append(put)

    latent_part(0)
    zero = (0,) * nb
    for stage in range(nb):
        absorb(out_copy, acc_o, rcv_o[stage], up, stage)
        if stage < nb - 1:
            out_copy = start(acc_o, snd_o, rcv_o[stage + 1], up, stage + 1)
        for k in range(nz):
            for h, order in enumerate((up, down)):
                absorb(moves[k][h], acc.at[k, h], rcv[stage].at[k, h], order, stage)
                if stage < nb - 1:
                    moves[k][h] = start(acc.at[k, h], snd.at[k, h], rcv[stage + 1].at[k, h], order, stage + 1)
            if stage == nb - 1 and k < nz - 1:
                zsnd[k] = acc[(k, slice(None)) + zero].astype(BF16)
                peer = {"grid": chip_at(k) * 2 + core}
                moves[k] = remote(zsnd.at[k], zrcv.at[k], peer)
        if stage == nb - 1:
            out_moves = []
            for k in range(nz - 1):
                zsnd_o[k] = acc_o[zero + (k,)].astype(BF16)
                peer = {"grid": chip_at(k) * 2 + core}
                out_moves.append(remote(zsnd_o.at[k], zrcv_o.at[k], peer))
        if stage == 0:
            latent_part(1)
            latent_part(2)
            latent_part(3)

    ratio = float(1.0 / np.sqrt(np.float32(ng * s.pts) * np.float32(n)))
    block = acc_o[zero + (nz - 1,)]
    for k in range(nz - 1):
        out_moves[k].wait_recv()
        block = block + zrcv_o[k].astype(F32)
    gall[mine, :] = ratio * block
    gathers = [remote(gall.at[mine], gall.at[mine], ens_peers[r]) for r in range(1, n)]
    block = acc[(nz - 1, slice(None)) + zero]
    for k in range(nz - 1):
        moves[k].wait_recv()
        block = block + zrcv[k].astype(F32)
    gin_ref[...] = (ratio * block).reshape(s.rows_e, s.cols)
    for copy in loss_copies:
        copy.wait_recv()
    loss = loss_g[0]
    for o in range(1, ng):
        loss = loss + loss_g[o]
    loss_ref[...] = loss[0:1, 0:1] * scale
    for copy in gathers:
        copy.wait_recv()
    gout_ref[...] = gall[0:s.nvars, :]
    for copy in sent:
        copy.wait_send()
    for put in puts:
        put.wait()


def per_device(n, ng, latent, w_in, w_out, target, area, var_weight):
    hid, lat = w_in.shape
    pts = latent.shape[2]
    nvars = w_out.shape[0]
    s = Sizes(n, ng, hid, lat, nvars, pts)
    nz, nb, cols = s.nz, s.nb, s.cols
    cube = (2,) * nb
    vmem = pl.BlockSpec(memory_space=pltpu.VMEM)
    anywhere = pl.BlockSpec(memory_space=pl.ANY)
    scratch = [
        pltpu.VMEM((nz, 2, cols, pts), BF16),
        pltpu.VMEM((nz, cols, pts), BF16),
        pltpu.VMEM((hid, lat), BF16),
        pltpu.VMEM((s.vpad, hid), F32),
        pltpu.VMEM((s.vpad, hid), BF16),
        pltpu.VMEM((hid, s.vpad), BF16),
        pltpu.VMEM((nz, 2, cols, pts), BF16),
        pltpu.VMEM((nz, cols, pts), BF16),
        pltpu.VMEM((hid, pts), F32),
        pltpu.VMEM((n, s.vrow, pts), F32),
        pltpu.VMEM((n, s.vrow, pts), F32),
        pltpu.VMEM((s.vpad, pts), F32),
        pltpu.VMEM((8, s.vpad), F32),
        pltpu.VMEM((s.vpad, 128), F32),
        pltpu.VMEM((ng, 8, pts), F32),
        pltpu.VMEM((n, s.vrow, pts), BF16),
        pltpu.VMEM((n, s.vrow, pts), BF16),
        pltpu.VMEM((n, s.vrow, pts), BF16),
        pltpu.VMEM((n, 8, 128), F32),
        pltpu.VMEM((ng, 8, 128), F32),
        pltpu.VMEM((hid, pts), BF16),
        pltpu.VMEM((hid, pts), BF16),
        pltpu.VMEM((lat, pts), BF16),
        pltpu.VMEM((s.vpad, cols), F32),
        pltpu.VMEM((nz, 2) + cube + (s.half, cols), F32),
        pltpu.VMEM((nz, 2) + cube + (s.half, cols), BF16),
        pltpu.VMEM(cube + (nz, s.vrow, cols), F32),
        pltpu.VMEM(cube + (nz, s.vrow, cols), BF16),
        pltpu.VMEM((n, s.vrow, cols), F32),
        pltpu.VMEM((nz - 1, 2, s.half, cols), BF16),
        pltpu.VMEM((nz - 1, 2, s.half, cols), BF16),
        pltpu.VMEM((nz - 1, s.vrow, cols), BF16),
        pltpu.VMEM((nz - 1, s.vrow, cols), BF16),
    ]
    scratch += [pltpu.VMEM((nz, 2) + cube[1 + i:] + (s.half, cols), BF16) for i in range(nb)]
    scratch += [pltpu.VMEM(cube[1 + i:] + (nz, s.vrow, cols), BF16) for i in range(nb)]
    scratch += [
        pltpu.SemaphoreType.DMA((s.copies,)),
        pltpu.SemaphoreType.DMA((s.copies,)),
        pltpu.SemaphoreType.DMA((6,)),
    ]
    loss, grad_lat, grad_in, grad_out = pl.pallas_call(
        functools.partial(kernel, s),
        out_shape=(
            jax.ShapeDtypeStruct((1, 1), F32),
            jax.ShapeDtypeStruct((1, lat, pts), BF16),
            jax.ShapeDtypeStruct((s.rows_e, cols), F32),
            jax.ShapeDtypeStruct((nvars, cols), F32),
        ),
        in_specs=[anywhere, anywhere, vmem, vmem, vmem, vmem],
        out_specs=(vmem, anywhere, vmem, vmem),
        scratch_shapes=scratch,
        compiler_params=pltpu.CompilerParams(
            collective_id=0, has_side_effects=True, vmem_limit_bytes=48 * 1024 * 1024
        ),
        name="crps_backward",
    )(latent.reshape(nz, 2, cols, pts), w_in, w_out, target, area, var_weight)
    return loss[0, 0], grad_lat, grad_in, grad_out


def solution(mesh):
    in_specs = (P("ens", None, "grid"), P(), P(), P(None, "grid"), P("grid"), P())
    out_specs = (P(), P("ens", None, "grid"), P("ens", "grid"), P(None, "grid"))
    body = functools.partial(per_device, mesh.shape["ens"], mesh.shape["grid"])
    return jax.shard_map(
        body, mesh=mesh, in_specs=in_specs, out_specs=out_specs, check_vma=False
    )
```

time: 154 us -> 51.4 us (0.33)
  blocking collectives: 83.3 us -> 0 us
  Pallas kernels: 0 us -> 40.8 us
  waiting for transfers between devices: 31.9 us -> 0 us
  between operations: 16.3 us -> 2.47 us
  matrix products: 8.39 us -> 0 us
  other arithmetic: 5.41 us -> 0 us
    psum x3 -> x0, blocking collectives: 73.7 us -> none  [the longest x1 38.1 us: per_device(): lax.psum(jnp.sum(weight * local), ('ens', 'grid')) / (weight_total * VARS)]
    pallas_call x0 -> x1, Pallas kernels: none -> 40.8 us  [per_device(): pl.pallas_call(functools.partial(kernel, s), out_shape=(jax.ShapeDtypeStr...]
    unnamed x5 -> x0, waiting for transfers between devices: 31.9 us -> none
    all_gather x1 -> x0, blocking collectives: 9.66 us -> none  [per_device(): lax.all_gather(decoded[None], 'ens', axis=0, tiled=True)]
    dot_general x6 -> x0, matrix products: 8.39 us -> none  [the longest x1 2.9 us: per_device(): preact = jnp.dot(w_in, features, preferred_element_type=jnp.float32)]
    mul x2 -> x0, other arithmetic: 2.2 us -> none  [per_device(): return (loss, grad_lat[None], ratio * total_in, ratio * total_out)]
    reduce_sum x2 -> x0, other arithmetic: 1.67 us -> none  [the longest x1 1.42 us: per_device(): weight_total = lax.psum(jnp.sum(area), 'grid')]
    convert_element_type x2 -> x0, other arithmetic: 1.54 us -> none  [the longest x1 0.83 us: per_device(): part_in = lax.psum_scatter(term_in.astype(jnp.bfloat16), 'grid', scatter_...]
  transfers between devices with their start and end apart: 3 -> 0, of which waited for: 1 -> 0; matrix products, arithmetic and copies ran while one was open for 4% -> 0% of each run, Pallas kernels for 0% -> 0%
where the time goes in v1:
time: 51.4 us; the launch traced here: 51.2 us
  Pallas kernels  40.8 us (79%)
  local copies, waits for them, and re-layouts  7.86 us (15%)
  between operations  2.47 us (5%)
    pallas_call x1, Pallas kernels, per_device(): pl.pallas_call(functools.partial(kernel, s), out_shape=(jax.ShapeDtypeStr...  40.8 us
    unnamed x15, local copies, waits for them, and re-layouts  7.86 us

profile of v1, /device:TPU:0, one launch (start us, length us, event | category | flops | bytes accessed | tf_op | source)
XLA Modules:
  0.0 51.2 jit_solution(18253093726748443101)
XLA Ops:
  0.6 0.0 copy-start
  0.6 1.6 %copy-done = bf16[1024,1024]{1,0:T(8,128)(2,1)S(1)} copy-done((bf16[1024,1024]{1,0:T(8,128)(2,1)S(1)}, bf16[1024,1024]{1,0:T(8,128)(2,1)}, u32[]{:S(2)}) %copy-start) | copy-done | bytes 2097176
  2.2 0.0 copy-start.1
  2.2 1.0 %copy-done.1 = bf16[1,1024,256]{2,1,0:T(8,128)(2,1)S(1)} copy-done((bf16[1,1024,256]{2,1,0:T(8,128)(2,1)S(1)}, bf16[1,1024,256]{2,1,0:T(8,128)(2,1)}, u32[]{:S(2)}) %copy-start.1) | copy-done | bytes 524312
  3.3 0.0 copy-start.2
  3.3 0.9 %copy-done.2 = bf16[99,1024]{1,0:T(8,128)(2,1)S(1)} copy-done((bf16[99,1024]{1,0:T(8,128)(2,1)S(1)}, bf16[99,1024]{1,0:T(8,128)(2,1)}, u32[]{:S(2)}) %copy-start.2) | copy-done | bytes 202776
  4.2 0.0 copy-start.3
  4.2 0.9 %copy-done.3 = f32[99,256]{1,0:T(8,128)S(1)} copy-done((f32[99,256]{1,0:T(8,128)S(1)}, f32[99,256]{1,0:T(8,128)}, u32[]{:S(2)}) %copy-start.3) | copy-done | bytes 101400
  5.1 0.0 copy-start.4
  5.1 0.7 %copy-done.4 = f32[256]{0:T(256)S(1)} copy-done((f32[256]{0:T(256)S(1)}, f32[256]{0:T(256)}, u32[]{:S(2)}) %copy-start.4) | copy-done | bytes 1048
  5.8 0.0 copy-start.5
  5.8 0.7 %copy-done.5 = f32[99]{0:T(128)S(1)} copy-done((f32[99]{0:T(128)S(1)}, f32[99]{0:T(128)}, u32[]{:S(2)}) %copy-start.5) | copy-done | bytes 420
  6.4 40.8 %crps_backward.1 = (f32[1,1]{1,0:T(1,128)}, bf16[1,1024,256]{2,1,0:T(8,128)(2,1)S(1)}, f32[256,128]{1,0:T(8,128)S(1)}, f32[99,128]{1,0:T(8,128)S(1)}) custom-call(bf16[4,2,128,256]{3,2,1,0:T(8,128)(2,1)S(1)} %bitcast.2, bf16[1024,1024]{1,0:T(8,128)(2,1)S(1)} %copy-done, bf16[99,1024]{1,0:T(8,128)(2,1)S(1)} %copy-done.2, f32[99,256]{1,0:T(8,128)S(1)} %copy-done.3, ...), custom_call_target="tpu_custom_call" | custom-call | tf_op jit(solution)/shard_map/crps_backward/pallas_call | solution.py:353
  48.0 0.8 %copy.15 = bf16[1,1024,256]{2,1,0:T(8,128)(2,1)} copy(bf16[1,1024,256]{2,1,0:T(8,128)(2,1)S(1)} %get-tuple-element.17) | data formatting | bytes 1048576
  48.7 0.7 %copy.16 = f32[256,128]{1,0:T(8,128)} copy(f32[256,128]{1,0:T(8,128)S(1)} %get-tuple-element.18) | data formatting | bytes 262144
  49.4 0.6 %copy.17 = f32[99,128]{1,0:T(8,128)} copy(f32[99,128]{1,0:T(8,128)S(1)} %get-tuple-element.19) | data formatting | bytes 101376
Async XLA Ops:
  0.6 1.6 %copy-start = (bf16[1024,1024]{1,0:T(8,128)(2,1)S(1)}, bf16[1024,1024]{1,0:T(8,128)(2,1)}, u32[]{:S(2)}) copy-start(bf16[1024,1024]{1,0:T(8,128)(2,1)} %win_hbm.1) | copy-start | bytes 6291460
  2.2 1.0 %copy-start.1 = (bf16[1,1024,256]{2,1,0:T(8,128)(2,1)S(1)}, bf16[1,1024,256]{2,1,0:T(8,128)(2,1)}, u32[]{:S(2)}) copy-start(bf16[1,1024,256]{2,1,0:T(8,128)(2,1)} %param.6) | copy-start | bytes 1572868
  3.3 0.9 %copy-start.2 = (bf16[99,1024]{1,0:T(8,128)(2,1)S(1)}, bf16[99,1024]{1,0:T(8,128)(2,1)}, u32[]{:S(2)}) copy-start(bf16[99,1024]{1,0:T(8,128)(2,1)} %wout_ref.1) | copy-start | bytes 608260
  4.2 0.9 %copy-start.3 = (f32[99,256]{1,0:T(8,128)S(1)}, f32[99,256]{1,0:T(8,128)}, u32[]{:S(2)}) copy-start(f32[99,256]{1,0:T(8,128)} %target_ref.1) | copy-start | bytes 304132
  5.1 0.7 %copy-start.4 = (f32[256]{0:T(256)S(1)}, f32[256]{0:T(256)}, u32[]{:S(2)}) copy-start(f32[256]{0:T(256)} %area_ref.1) | copy-start | bytes 3076
  5.8 0.7 %copy-start.5 = (f32[99]{0:T(128)S(1)}, f32[99]{0:T(128)}, u32[]{:S(2)}) copy-start(f32[99]{0:T(128)} %vw_ref.1) | copy-start | bytes 1192

commit v2 on v1

--- a/solution.py
+++ b/solution.py
@@ -13,6 +13,7 @@
 GELU_K = 0.044715
 F32 = jnp.float32
 BF16 = jnp.bfloat16
+VMEM_BYTES = 62 * 1024 * 1024
 
 
 def dot_nn(a, b):
@@ -52,11 +53,11 @@
 
 def kernel(
     s,
-    lat_hbm, win_hbm, wout_ref, target_ref, area_ref, vw_ref,
+    lat_hbm, win_hbm, wout_hbm, target_hbm, area_ref, vw_ref,
     loss_ref, glat_hbm, gin_ref, gout_ref,
-    lat_s, latp, win_s, wo32, wo_s, wot, hid_s, hidp, slope_s, dec_s, dec_in, tgt_s, vrow_s, vcol_s, area_all,
+    lat_s, latp, win_s, wint, wout_ref, target_ref, wo32, wo_s, wot, hid_s, hidp, slope_s, dec_s, dec_in, tgt_s, vrow_s, vcol_s, area_all,
     dout_o, dout_s, doutp, loss_e, loss_g, dpre_s, dprep, glat_s, gall,
-    acc, snd, acc_o, snd_o, tmp_o, zsnd, zrcv, zsnd_o, zrcv_o, *rest,
+    tmp, acc, snd, acc_o, snd_o, tmp_o, zsnd, zrcv, zsnd_o, zrcv_o, *rest,
 ):
     nb, n, ng, nz = s.nb, s.n, s.ng, s.nz
     rcv, rcv_o = rest[:nb], rest[nb:2 * nb]
@@ -87,34 +88,35 @@
     ens_peers = [None] + [{"ens": ens_peer(r)} for r in range(1, n)]
     grid_peers = [None] + [{"grid": (g + o) % ng} for o in range(1, ng)]
 
+    def win_tile(i):
+        rows = pl.ds(pl.multiple_of(i * s.tile, s.tile), s.tile)
+        return pltpu.make_async_copy(win_hbm.at[rows], win_s.at[rows], local_sem.at[3 + i])
+
     get_lat = pltpu.make_async_copy(lat_hbm, lat_s, local_sem.at[0])
-    get_win = pltpu.make_async_copy(win_hbm, win_s, local_sem.at[1])
+    get_out = pltpu.make_async_copy(wout_hbm, wout_ref, local_sem.at[1])
+    get_target = pltpu.make_async_copy(target_hbm, target_ref, local_sem.at[2])
     get_lat.start()
-    get_win.start()
+    for i in range(s.tiles):
+        win_tile(i).start()
+    get_out.start()
+    get_target.start()
     barrier = pltpu.get_barrier_semaphore()
     for peer in ens_peers[1:] + grid_peers[1:]:
         pl.semaphore_signal(barrier, inc=1, device_id=peer, device_id_type=pl.DeviceIdType.MESH)
 
     arow = area_ref[...].reshape(1, s.pts)
-    area_all[0] = jnp.broadcast_to(arow, (8, s.pts))
-    wo32[...] = jnp.zeros_like(wo32)
-    wo32[0:s.nvars, :] = wout_ref[...].astype(F32)
-    wo_s[...] = wo32[...].astype(BF16)
-    tgt_s[...] = jnp.zeros_like(tgt_s)
-    tgt_s[0:s.nvars, :] = target_ref[...]
+    area_all[0] = jnp.broadcast_to(jnp.sum(arow, axis=1, keepdims=True), (8, 128))
     vrow_s[...] = jnp.zeros_like(vrow_s)
     vrow_s[0:1, 0:s.nvars] = vw_ref[...].reshape(1, s.nvars)
-
-    pl.semaphore_wait(barrier, n + ng - 2)
-    lat_copy = remote(lat_hbm.at[:, 1 - core], latp, twin)
-    area_copies = [remote(area_all.at[0], area_all.at[o], grid_peers[o]) for o in range(1, ng)]
+    wo32[...] = jnp.zeros_like(wo32)
+    tgt_s[...] = jnp.zeros_like(tgt_s)
 
     get_lat.wait()
-    get_win.wait()
     span = s.tile // (2 * s.cols)
 
     def forward(i, carry):
         rows = pl.ds(pl.multiple_of(i * s.tile, s.tile), s.tile)
+        win_tile(i).wait()
         v = dot_nn(win_s[rows, :], lat_s[...].reshape(s.lat, s.pts))
         t = jnp.tanh(GELU_C * (v + GELU_K * v * v * v))
         hid_s[pl.ds(i * span, span)] = (0.5 * v * (1.0 + t)).astype(BF16).reshape(span, 2, s.cols, s.pts)
@@ -122,11 +124,19 @@
         return carry
 
     lax.fori_loop(0, s.tiles, forward, 0)
+    get_out.wait()
+    wo32[0:s.nvars, :] = wout_ref[...].astype(F32)
+    wo_s[...] = wo32[...].astype(BF16)
     dec_s[...] = dot_nn(wo_s[...], hid_s[...].reshape(s.hid, s.pts)).reshape(n, s.vrow, s.pts)
+    pl.semaphore_wait(barrier, n + ng - 2)
 
     dec_copies = [remote(dec_s.at[ens_peer(r)], dec_in.at[r], ens_peers[r]) for r in range(1, n)]
+    area_copies = [remote(area_all.at[0], area_all.at[o], grid_peers[o]) for o in range(1, ng)]
     hid_copy = remote(hid_s.at[:, 1 - core], hidp, twin)
+    lat_copy = remote(lat_hbm.at[:, 1 - core], latp, twin)
     dec_in[0] = dec_s[me]
+    get_target.wait()
+    tgt_s[0:s.nvars, :] = target_ref[...]
     wot[...] = wo32[...].T.astype(BF16)
     square = (s.vpad, s.vpad)
     eye = lax.broadcasted_iota(jnp.int32, square, 0) == lax.broadcasted_iota(jnp.int32, square, 1)
@@ -135,10 +145,20 @@
     mine = pl.ds(pl.multiple_of(me * s.vrow, s.vrow), s.vrow)
     weight = vcol_s[mine, 0:1] * arow
     target = tgt_s[mine, :]
+    turned = s.lat // 4
+
+    def turn(j):
+        at = pl.ds(j * turned, turned)
+        wint[at, :] = win_s[:, at].T
+
+    turn(0)
+    turn(1)
     for copy in area_copies:
         copy.wait_recv()
-    total = jnp.sum(area_all[...][:, 0, :].reshape(ng, s.pts), axis=1, keepdims=True)
-    total = jnp.sum(total, axis=0, keepdims=True)
+    total = area_all[0]
+    for o in range(1, ng):
+        total = total + area_all[o]
+    total = total[0:1, 0:1]
     scale = 1.0 / (total * float(s.nvars))
     wide = (float(ng * s.pts) * scale) * weight
     for copy in dec_copies:
@@ -172,6 +192,8 @@
     loss_e[0] = jnp.broadcast_to(part, (8, 128))
     loss_copies = [remote(loss_e.at[0], loss_e.at[r], ens_peers[r]) for r in range(1, n)]
 
+    turn(2)
+    turn(3)
     for copy in dout_copies:
         copy.wait_recv()
     dout_copy = remote(dout_s, doutp, twin)
@@ -190,11 +212,17 @@
     def relative(r):
         return tuple((r >> (nb - 1 - axis)) & 1 for axis in range(nb))
 
+    def place(value, sums, send, at, r, order):
+        if (r >> order[0]) & 1:
+            send[at] = value.astype(BF16)
+        else:
+            sums[at] = value
+
     def start(sums, send, into, order, stage):
         index = stage_index(nb, order, stage, 1)
-        send[index] = sums[index].astype(BF16)
-        bit = order[stage]
-        return remote(send.at[index], into, ens_peers[1 << bit])
+        if stage:
+            send[index] = sums[index].astype(BF16)
+        return remote(send.at[index], into, ens_peers[1 << order[stage]])
 
     def absorb(copy, sums, into, order, stage):
         copy.wait_recv()
@@ -211,66 +239,84 @@
 
     hid_copy.wait_recv()
     dout_copy.wait_recv()
-    for k in range(nz):
-        z = chip_at(k)
-        term = dot_nt(dout, hid_s[z, core]) + dot_nt(doutp[...].reshape(s.vpad, s.pts), hidp[z])
-        tmp_o[...] = term.reshape(n, s.vrow, s.cols)
+    group = max(1, min(nz, 256 // s.cols))
+    wide_rows = (group * s.cols, s.pts)
+    doutp_all = doutp[...].reshape(s.vpad, s.pts)
+    for first in range(0, nz, group):
+        zs = [chip_at(k) for k in range(first, first + group)]
+        own = jnp.stack([hid_s[z, core] for z in zs]).reshape(wide_rows)
+        other = jnp.stack([hidp[z] for z in zs]).reshape(wide_rows)
+        tmp_o[...] = (dot_nt(dout, own) + dot_nt(doutp_all, other)).reshape(n, s.vrow, group * s.cols)
         for r in range(n):
-            acc_o[relative(r) + (k,)] = tmp_o[ens_peer(r)]
+            for k in range(group):
+                value = tmp_o[ens_peer(r), :, k * s.cols:(k + 1) * s.cols]
+                place(value, acc_o, snd_o, relative(r) + (first + k,), r, up)
     out_copy = start(acc_o, snd_o, rcv_o[0], up, 0)
 
+    moves = [None] * nz
+    orders = (up, down)
     lat_copy.wait_recv()
-    for copy in dpre_copies:
-        copy.wait_recv()
-    moves = []
-    for k in range(nz):
-        z = chip_at(k)
-        own, other = lat_s[z, core], latp[z]
-        for r in range(n):
-            rows = pl.ds(pl.multiple_of(ens_peer(r) * s.rows_e, s.rows_e), s.rows_e)
-            term = dot_nt(dpre_s[rows, :], own) + dot_nt(dprep[rows, :], other)
-            acc[(k, 0) + relative(r)] = term[:s.half]
-            acc[(k, 1) + relative(r)] = term[s.half:]
-        moves.append([
-            start(acc.at[k, h], snd.at[k, h], rcv[0].at[k, h], order, 0)
-            for h, order in enumerate((up, down))
-        ])
-
-    width = s.lat // 4
+    for first in range(0, nz, group):
+        zs = [chip_at(k) for k in range(first, first + group)]
+        own = jnp.stack([lat_s[z, core] for z in zs]).reshape(wide_rows)
+        other = jnp.stack([latp[z] for z in zs]).reshape(wide_rows)
+        for i in range(s.tiles):
+            rows = pl.ds(i * s.tile, s.tile)
+            tmp[rows, :] = dot_nt(dpre_s[rows, :], own)
+        for i in range(s.tiles):
+            if first == 0:
+                dpre_copies[i].wait_recv()
+            rows = pl.ds(i * s.tile, s.tile)
+            tmp[rows, :] += dot_nt(dprep[rows, :], other)
+        for k in range(first, first + group):
+            lanes = slice((k - first) * s.cols, (k - first + 1) * s.cols)
+            for r in range(n):
+                for h in range(2):
+                    base = ens_peer(r) * s.rows_e + h * s.half
+                    value = tmp[pl.ds(pl.multiple_of(base, s.half), s.half), lanes]
+                    place(value, acc, snd, (k, h) + relative(r), r, orders[h])
+            moves[k] = [start(acc.at[k, h], snd.at[k, h], rcv[0].at[k, h], orders[h], 0) for h in range(2)]
+
     puts = []
 
     def latent_part(j):
-        at = pl.ds(j * width, width)
-        glat_s[at, :] = dot_tn(win_s[:, at], dpre_s[...]).astype(BF16)
-        put = pltpu.make_async_copy(glat_s.at[at], glat_hbm.at[0, at], local_sem.at[2 + j])
+        at = pl.ds(j * turned, turned)
+        glat_s[at, :] = dot_nn(wint[at, :], dpre_s[...]).astype(BF16)
+        put = pltpu.make_async_copy(glat_s.at[at], glat_hbm.at[0, at], local_sem.at[3 + s.tiles + j])
         put.start()
         puts.append(put)
 
     latent_part(0)
+    latent_part(1)
     zero = (0,) * nb
-    for stage in range(nb):
-        absorb(out_copy, acc_o, rcv_o[stage], up, stage)
+    out_moves = []
+
+    def out_step(copy, stage):
+        absorb(copy, acc_o, rcv_o[stage], up, stage)
         if stage < nb - 1:
-            out_copy = start(acc_o, snd_o, rcv_o[stage + 1], up, stage + 1)
-        for k in range(nz):
-            for h, order in enumerate((up, down)):
+            return start(acc_o, snd_o, rcv_o[stage + 1], up, stage + 1)
+        for k in range(nz - 1):
+            zsnd_o[k] = acc_o[zero + (k,)].astype(BF16)
+            out_moves.append(remote(zsnd_o.at[k], zrcv_o.at[k], {"grid": chip_at(k) * 2 + core}))
+        return None
+
+    out_copy = out_step(out_copy, 0)
+    latent_part(2)
+    latent_part(3)
+    for step in range(nz + nb - 1):
+        for stage in range(nb):
+            k = step - stage
+            if not 0 <= k < nz:
+                continue
+            for h, order in enumerate(orders):
                 absorb(moves[k][h], acc.at[k, h], rcv[stage].at[k, h], order, stage)
                 if stage < nb - 1:
                     moves[k][h] = start(acc.at[k, h], snd.at[k, h], rcv[stage + 1].at[k, h], order, stage + 1)
             if stage == nb - 1 and k < nz - 1:
                 zsnd[k] = acc[(k, slice(None)) + zero].astype(BF16)
-                peer = {"grid": chip_at(k) * 2 + core}
-                moves[k] = remote(zsnd.at[k], zrcv.at[k], peer)
-        if stage == nb - 1:
-            out_moves = []
-            for k in range(nz - 1):
-                zsnd_o[k] = acc_o[zero + (k,)].astype(BF16)
-                peer = {"grid": chip_at(k) * 2 + core}
-                out_moves.append(remote(zsnd_o.at[k], zrcv_o.at[k], peer))
-        if stage == 0:
-            latent_part(1)
-            latent_part(2)
-            latent_part(3)
+                moves[k] = remote(zsnd.at[k], zrcv.at[k], {"grid": chip_at(k) * 2 + core})
+        if step + 1 < nb:
+            out_copy = out_step(out_copy, step + 1)
 
     ratio = float(1.0 / np.sqrt(np.float32(ng * s.pts) * np.float32(n)))
     block = acc_o[zero + (nz - 1,)]
@@ -299,6 +345,14 @@
         put.wait()
 
 
+def hand_out(a, b, c, a_out, b_out, c_out, sem):
+    copies = [pltpu.make_async_copy(x, y, sem.at[i]) for i, (x, y) in enumerate(((a, a_out), (b, b_out), (c, c_out)))]
+    for copy in copies:
+        copy.start()
+    for copy in copies:
+        copy.wait()
+
+
 def per_device(n, ng, latent, w_in, w_out, target, area, var_weight):
     hid, lat = w_in.shape
     pts = latent.shape[2]
@@ -306,12 +360,16 @@
     s = Sizes(n, ng, hid, lat, nvars, pts)
     nz, nb, cols = s.nz, s.nb, s.cols
     cube = (2,) * nb
+    group = max(1, min(nz, 256 // cols))
     vmem = pl.BlockSpec(memory_space=pltpu.VMEM)
     anywhere = pl.BlockSpec(memory_space=pl.ANY)
     scratch = [
         pltpu.VMEM((nz, 2, cols, pts), BF16),
         pltpu.VMEM((nz, cols, pts), BF16),
         pltpu.VMEM((hid, lat), BF16),
+        pltpu.VMEM((lat, hid), BF16),
+        pltpu.VMEM((nvars, hid), BF16),
+        pltpu.VMEM((nvars, pts), F32),
         pltpu.VMEM((s.vpad, hid), F32),
         pltpu.VMEM((s.vpad, hid), BF16),
         pltpu.VMEM((hid, s.vpad), BF16),
@@ -323,7 +381,7 @@
         pltpu.VMEM((s.vpad, pts), F32),
         pltpu.VMEM((8, s.vpad), F32),
         pltpu.VMEM((s.vpad, 128), F32),
-        pltpu.VMEM((ng, 8, pts), F32),
+        pltpu.VMEM((ng, 8, 128), F32),
         pltpu.VMEM((n, s.vrow, pts), BF16),
         pltpu.VMEM((n, s.vrow, pts), BF16),
         pltpu.VMEM((n, s.vrow, pts), BF16),
@@ -333,11 +391,12 @@
         pltpu.VMEM((hid, pts), BF16),
         pltpu.VMEM((lat, pts), BF16),
         pltpu.VMEM((s.vpad, cols), F32),
+        pltpu.VMEM((hid, group * cols), F32),
         pltpu.VMEM((nz, 2) + cube + (s.half, cols), F32),
         pltpu.VMEM((nz, 2) + cube + (s.half, cols), BF16),
         pltpu.VMEM(cube + (nz, s.vrow, cols), F32),
         pltpu.VMEM(cube + (nz, s.vrow, cols), BF16),
-        pltpu.VMEM((n, s.vrow, cols), F32),
+        pltpu.VMEM((n, s.vrow, group * cols), F32),
         pltpu.VMEM((nz - 1, 2, s.half, cols), BF16),
         pltpu.VMEM((nz - 1, 2, s.half, cols), BF16),
         pltpu.VMEM((nz - 1, s.vrow, cols), BF16),
@@ -348,7 +407,7 @@
     scratch += [
         pltpu.SemaphoreType.DMA((s.copies,)),
         pltpu.SemaphoreType.DMA((s.copies,)),
-        pltpu.SemaphoreType.DMA((6,)),
+        pltpu.SemaphoreType.DMA((7 + s.tiles,)),
     ]
     loss, grad_lat, grad_in, grad_out = pl.pallas_call(
         functools.partial(kernel, s),
@@ -358,14 +417,23 @@
             jax.ShapeDtypeStruct((s.rows_e, cols), F32),
             jax.ShapeDtypeStruct((nvars, cols), F32),
         ),
-        in_specs=[anywhere, anywhere, vmem, vmem, vmem, vmem],
+        in_specs=[anywhere, anywhere, anywhere, anywhere, vmem, vmem],
         out_specs=(vmem, anywhere, vmem, vmem),
         scratch_shapes=scratch,
         compiler_params=pltpu.CompilerParams(
-            collective_id=0, has_side_effects=True, vmem_limit_bytes=48 * 1024 * 1024
+            collective_id=0, has_side_effects=True, vmem_limit_bytes=VMEM_BYTES
         ),
         name="crps_backward",
     )(latent.reshape(nz, 2, cols, pts), w_in, w_out, target, area, var_weight)
+    grad_lat, grad_in, grad_out = pl.pallas_call(
+        hand_out,
+        out_shape=tuple(jax.ShapeDtypeStruct(x.shape, x.dtype) for x in (grad_lat, grad_in, grad_out)),
+        in_specs=[anywhere] * 3,
+        out_specs=(anywhere,) * 3,
+        scratch_shapes=[pltpu.SemaphoreType.DMA((3,))],
+        compiler_params=pltpu.CompilerParams(vmem_limit_bytes=VMEM_BYTES),
+        name="hand_out",
+    )(grad_lat, grad_in, grad_out)
     return loss[0, 0], grad_lat, grad_in, grad_out
 
 

time: 51.4 us -> 62.7 us (1.22)
  Pallas kernels: 40.8 us -> 60.1 us
  local copies, waits for them, and re-layouts: 7.86 us -> 0 us
    pallas_call x0 -> x1, Pallas kernels: none -> 22.5 us  [per_device(): pl.pallas_call(hand_out, out_shape=tuple((jax.ShapeDtypeStruct(x.shape, x...]
    unnamed x15 -> x0, local copies, waits for them, and re-layouts: 7.86 us -> none
    pallas_call x1, Pallas kernels: 40.8 us -> 37.6 us  [per_device(): pl.pallas_call(functools.partial(kernel, s), out_shape=(jax.ShapeDtypeStr...]
where the time goes in v2:
time: 62.7 us; the launch traced here: 62.6 us
  Pallas kernels  60.1 us (96%)
  between operations  2.44 us (4%)
    pallas_call x1, Pallas kernels, per_device(): pl.pallas_call(functools.partial(kernel, s), out_shape=(jax.ShapeDtypeStr...  37.6 us
    pallas_call x1, Pallas kernels, per_device(): pl.pallas_call(hand_out, out_shape=tuple((jax.ShapeDtypeStruct(x.shape, x...  22.5 us

profile of v2, /device:TPU:0, one launch (start us, length us, event | category | flops | bytes accessed | tf_op | source)
XLA Modules:
  0.0 62.6 jit_solution(12115566439500261499)
XLA Ops:
  0.6 37.6 %crps_backward.1 = (f32[1,1]{1,0:T(1,128)}, bf16[1,1024,256]{2,1,0:T(8,128)(2,1)}, f32[256,128]{1,0:T(8,128)}, f32[99,128]{1,0:T(8,128)}) custom-call(bf16[4,2,128,256]{3,2,1,0:T(8,128)(2,1)} %bitcast.2, bf16[1024,1024]{1,0:T(8,128)(2,1)} %win_hbm.1, bf16[99,1024]{1,0:T(8,128)(2,1)} %wout_hbm.1, f32[99,256]{1,0:T(8,128)} %target_hbm.1, f32[256]{0:T(256)} %area_ref.1, ...), custom_call_target="tpu_custom_call" | custom-call | tf_op jit(solution)/shard_map/crps_backward/pallas_call | solution.py:412
  38.2 22.5 %hand_out.1 = (bf16[1,1024,256]{2,1,0:T(8,128)(2,1)}, f32[256,128]{1,0:T(8,128)}, f32[99,128]{1,0:T(8,128)}) custom-call(bf16[1,1024,256]{2,1,0:T(8,128)(2,1)} %get-tuple-element.12.a, f32[256,128]{1,0:T(8,128)} %get-tuple-element.13.b, f32[99,128]{1,0:T(8,128)} %get-tuple-element.14.c), custom_call_target="tpu_custom_call" | custom-call | tf_op jit(solution)/shard_map/hand_out/pallas_call | solution.py:428

commit v3 on v2

--- a/solution.py
+++ b/solution.py
@@ -53,10 +53,10 @@
 
 def kernel(
     s,
-    lat_hbm, win_hbm, wout_hbm, target_hbm, area_ref, vw_ref,
-    loss_ref, glat_hbm, gin_ref, gout_ref,
-    lat_s, latp, win_s, wint, wout_ref, target_ref, wo32, wo_s, wot, hid_s, hidp, slope_s, dec_s, dec_in, tgt_s, vrow_s, vcol_s, area_all,
-    dout_o, dout_s, doutp, loss_e, loss_g, dpre_s, dprep, glat_s, gall,
+    lat_hbm, win_hbm, wout_hbm, target_hbm, area_hbm, vw_hbm,
+    loss_ref, glat_ref, gin_ref, gout_ref,
+    lat_s, latp, win_s, wint, wout_ref, target_ref, area_ref, vw_ref, wo32, wo_s, wot, hid_s, hidp, slope_s, dec_s, dec_in, tgt_s, vrow_s, vcol_s, area_all,
+    dout_o, dout_s, doutp, loss_e, loss_g, dpre_s, dprep, gall,
     tmp, acc, snd, acc_o, snd_o, tmp_o, zsnd, zrcv, zsnd_o, zrcv_o, *rest,
 ):
     nb, n, ng, nz = s.nb, s.n, s.ng, s.nz
@@ -95,19 +95,20 @@
     get_lat = pltpu.make_async_copy(lat_hbm, lat_s, local_sem.at[0])
     get_out = pltpu.make_async_copy(wout_hbm, wout_ref, local_sem.at[1])
     get_target = pltpu.make_async_copy(target_hbm, target_ref, local_sem.at[2])
+    get_area = pltpu.make_async_copy(area_hbm, area_ref, local_sem.at[3 + s.tiles])
+    get_vw = pltpu.make_async_copy(vw_hbm, vw_ref, local_sem.at[4 + s.tiles])
     get_lat.start()
     for i in range(s.tiles):
         win_tile(i).start()
     get_out.start()
+    get_area.start()
+    get_vw.start()
     get_target.start()
     barrier = pltpu.get_barrier_semaphore()
     for peer in ens_peers[1:] + grid_peers[1:]:
         pl.semaphore_signal(barrier, inc=1, device_id=peer, device_id_type=pl.DeviceIdType.MESH)
 
-    arow = area_ref[...].reshape(1, s.pts)
-    area_all[0] = jnp.broadcast_to(jnp.sum(arow, axis=1, keepdims=True), (8, 128))
     vrow_s[...] = jnp.zeros_like(vrow_s)
-    vrow_s[0:1, 0:s.nvars] = vw_ref[...].reshape(1, s.nvars)
     wo32[...] = jnp.zeros_like(wo32)
     tgt_s[...] = jnp.zeros_like(tgt_s)
 
@@ -124,6 +125,11 @@
         return carry
 
     lax.fori_loop(0, s.tiles, forward, 0)
+    get_area.wait()
+    get_vw.wait()
+    arow = area_ref[...].reshape(1, s.pts)
+    area_all[0] = jnp.broadcast_to(jnp.sum(arow, axis=1, keepdims=True), (8, 128))
+    vrow_s[0:1, 0:s.nvars] = vw_ref[...].reshape(1, s.nvars)
     get_out.wait()
     wo32[0:s.nvars, :] = wout_ref[...].astype(F32)
     wo_s[...] = wo32[...].astype(BF16)
@@ -229,14 +235,6 @@
         index = stage_index(nb, order, stage, 0)
         sums[index] = sums[index] + into[...].astype(F32)
 
-    for copy in loss_copies:
-        copy.wait_recv()
-    here = loss_e[0]
-    for r in range(1, n):
-        here = here + loss_e[r]
-    loss_g[0] = here
-    loss_copies = [remote(loss_g.at[0], loss_g.at[o], grid_peers[o]) for o in range(1, ng)]
-
     hid_copy.wait_recv()
     dout_copy.wait_recv()
     group = max(1, min(nz, 256 // s.cols))
@@ -277,14 +275,10 @@
                     place(value, acc, snd, (k, h) + relative(r), r, orders[h])
             moves[k] = [start(acc.at[k, h], snd.at[k, h], rcv[0].at[k, h], orders[h], 0) for h in range(2)]
 
-    puts = []
 
     def latent_part(j):
         at = pl.ds(j * turned, turned)
-        glat_s[at, :] = dot_nn(wint[at, :], dpre_s[...]).astype(BF16)
-        put = pltpu.make_async_copy(glat_s.at[at], glat_hbm.at[0, at], local_sem.at[3 + s.tiles + j])
-        put.start()
-        puts.append(put)
+        glat_ref[0, at, :] = dot_nn(wint[at, :], dpre_s[...]).astype(BF16)
 
     latent_part(0)
     latent_part(1)
@@ -303,6 +297,14 @@
     out_copy = out_step(out_copy, 0)
     latent_part(2)
     latent_part(3)
+    for copy in loss_copies:
+        copy.wait_recv()
+    here = loss_e[0]
+    for r in range(1, n):
+        here = here + loss_e[r]
+    loss_g[0] = here
+    loss_copies = [remote(loss_g.at[0], loss_g.at[o], grid_peers[o]) for o in range(1, ng)]
+    ratio = float(1.0 / np.sqrt(np.float32(ng * s.pts) * np.float32(n)))
     for step in range(nz + nb - 1):
         for stage in range(nb):
             k = step - stage
@@ -317,14 +319,14 @@
                 moves[k] = remote(zsnd.at[k], zrcv.at[k], {"grid": chip_at(k) * 2 + core})
         if step + 1 < nb:
             out_copy = out_step(out_copy, step + 1)
-
-    ratio = float(1.0 / np.sqrt(np.float32(ng * s.pts) * np.float32(n)))
-    block = acc_o[zero + (nz - 1,)]
-    for k in range(nz - 1):
-        out_moves[k].wait_recv()
-        block = block + zrcv_o[k].astype(F32)
-    gall[mine, :] = ratio * block
-    gathers = [remote(gall.at[mine], gall.at[mine], ens_peers[r]) for r in range(1, n)]
+        if step == nz + nb - 3:
+            block = acc_o[zero + (nz - 1,)]
+            for k in range(nz - 1):
+                out_moves[k].wait_recv()
+                block = block + zrcv_o[k].astype(F32)
+            gall[mine, :] = ratio * block
+            gathers = [remote(gall.at[mine], gall.at[mine], ens_peers[r]) for r in range(1, n)]
+
     block = acc[(nz - 1, slice(None)) + zero]
     for k in range(nz - 1):
         moves[k].wait_recv()
@@ -341,8 +343,6 @@
     gout_ref[...] = gall[0:s.nvars, :]
     for copy in sent:
         copy.wait_send()
-    for put in puts:
-        put.wait()
 
 
 def hand_out(a, b, c, a_out, b_out, c_out, sem):
@@ -362,7 +362,7 @@
     cube = (2,) * nb
     group = max(1, min(nz, 256 // cols))
     vmem = pl.BlockSpec(memory_space=pltpu.VMEM)
-    anywhere = pl.BlockSpec(memory_space=pl.ANY)
+    hbm = pl.BlockSpec(memory_space=pltpu.HBM)
     scratch = [
         pltpu.VMEM((nz, 2, cols, pts), BF16),
         pltpu.VMEM((nz, cols, pts), BF16),
@@ -370,6 +370,8 @@
         pltpu.VMEM((lat, hid), BF16),
         pltpu.VMEM((nvars, hid), BF16),
         pltpu.VMEM((nvars, pts), F32),
+        pltpu.VMEM((pts,), F32),
+        pltpu.VMEM((nvars,), F32),
         pltpu.VMEM((s.vpad, hid), F32),
         pltpu.VMEM((s.vpad, hid), BF16),
         pltpu.VMEM((hid, s.vpad), BF16),
@@ -389,7 +391,6 @@
         pltpu.VMEM((ng, 8, 128), F32),
         pltpu.VMEM((hid, pts), BF16),
         pltpu.VMEM((hid, pts), BF16),
-        pltpu.VMEM((lat, pts), BF16),
         pltpu.VMEM((s.vpad, cols), F32),
         pltpu.VMEM((hid, group * cols), F32),
         pltpu.VMEM((nz, 2) + cube + (s.half, cols), F32),
@@ -407,7 +408,7 @@
     scratch += [
         pltpu.SemaphoreType.DMA((s.copies,)),
         pltpu.SemaphoreType.DMA((s.copies,)),
-        pltpu.SemaphoreType.DMA((7 + s.tiles,)),
+        pltpu.SemaphoreType.DMA((5 + s.tiles,)),
     ]
     loss, grad_lat, grad_in, grad_out = pl.pallas_call(
         functools.partial(kernel, s),
@@ -417,8 +418,8 @@
             jax.ShapeDtypeStruct((s.rows_e, cols), F32),
             jax.ShapeDtypeStruct((nvars, cols), F32),
         ),
-        in_specs=[anywhere, anywhere, anywhere, anywhere, vmem, vmem],
-        out_specs=(vmem, anywhere, vmem, vmem),
+        in_specs=[hbm] * 6,
+        out_specs=(vmem,) * 4,
         scratch_shapes=scratch,
         compiler_params=pltpu.CompilerParams(
             collective_id=0, has_side_effects=True, vmem_limit_bytes=VMEM_BYTES
@@ -428,8 +429,8 @@
     grad_lat, grad_in, grad_out = pl.pallas_call(
         hand_out,
         out_shape=tuple(jax.ShapeDtypeStruct(x.shape, x.dtype) for x in (grad_lat, grad_in, grad_out)),
-        in_specs=[anywhere] * 3,
-        out_specs=(anywhere,) * 3,
+        in_specs=[vmem] * 3,
+        out_specs=(hbm,) * 3,
         scratch_shapes=[pltpu.SemaphoreType.DMA((3,))],
         compiler_params=pltpu.CompilerParams(vmem_limit_bytes=VMEM_BYTES),
         name="hand_out",

time: 62.7 us -> 41.3 us (0.66)
  Pallas kernels: 60.1 us -> 38.7 us
    pallas_call x1, Pallas kernels: 22.5 us -> 1.98 us  [per_device(): pl.pallas_call(hand_out, out_shape=tuple((jax.ShapeDtypeStruct(x.shape, x...]
    pallas_call x1, Pallas kernels: 37.6 us -> 36.7 us  [per_device(): pl.pallas_call(functools.partial(kernel, s), out_shape=(jax.ShapeDtypeStr...]
where the time goes in v3:
time: 41.3 us; the launch traced here: 41.1 us
  Pallas kernels  38.7 us (94%)
  between operations  2.44 us (6%)
    pallas_call x1, Pallas kernels, per_device(): pl.pallas_call(functools.partial(kernel, s), out_shape=(jax.ShapeDtypeStr...  36.7 us
    pallas_call x1, Pallas kernels, per_device(): pl.pallas_call(hand_out, out_shape=tuple((jax.ShapeDtypeStruct(x.shape, x...  1.98 us

profile of v3, /device:TPU:0, one launch (start us, length us, event | category | flops | bytes accessed | tf_op | source)
XLA Modules:
  0.0 41.1 jit_solution(6403230779540499590)
XLA Ops:
  0.6 36.7 %crps_backward.1 = (f32[1,1]{1,0:T(1,128)}, bf16[1,1024,256]{2,1,0:T(8,128)(2,1)}, f32[256,128]{1,0:T(8,128)}, f32[99,128]{1,0:T(8,128)}) custom-call(bf16[4,2,128,256]{3,2,1,0:T(8,128)(2,1)} %bitcast.2, bf16[1024,1024]{1,0:T(8,128)(2,1)} %win_hbm.1, bf16[99,1024]{1,0:T(8,128)(2,1)} %wout_hbm.1, f32[99,256]{1,0:T(8,128)} %target_hbm.1, f32[256]{0:T(256)} %area_hbm.1, ...), custom_call_target="tpu_custom_call" | custom-call | tf_op jit(solution)/shard_map/crps_backward/pallas_call | solution.py:413
  37.3 2.0 %hand_out.1 = (bf16[1,1024,256]{2,1,0:T(8,128)(2,1)}, f32[256,128]{1,0:T(8,128)}, f32[99,128]{1,0:T(8,128)}) custom-call(bf16[1,1024,256]{2,1,0:T(8,128)(2,1)} %get-tuple-element.12.a, f32[256,128]{1,0:T(8,128)} %get-tuple-element.13.b, f32[99,128]{1,0:T(8,128)} %get-tuple-element.14.c), custom_call_target="tpu_custom_call" | custom-call | tf_op jit(solution)/shard_map/hand_out/pallas_call | solution.py:429

commit v4 on v3

--- a/solution.py
+++ b/solution.py
@@ -55,7 +55,7 @@
     s,
     lat_hbm, win_hbm, wout_hbm, target_hbm, area_hbm, vw_hbm,
     loss_ref, glat_ref, gin_ref, gout_ref,
-    lat_s, latp, win_s, wint, wout_ref, target_ref, area_ref, vw_ref, wo32, wo_s, wot, hid_s, hidp, slope_s, dec_s, dec_in, tgt_s, vrow_s, vcol_s, area_all,
+    lat_s, latp, win_s, wout_ref, target_ref, area_ref, vw_ref, wo32, wo_s, wot, hid_s, hidp, pre_s, slope_s, dec_s, dec_in, tgt_s, vrow_s, vcol_s, area_all,
     dout_o, dout_s, doutp, loss_e, loss_g, dpre_s, dprep, gall,
     tmp, acc, snd, acc_o, snd_o, tmp_o, zsnd, zrcv, zsnd_o, zrcv_o, *rest,
 ):
@@ -89,7 +89,7 @@
     grid_peers = [None] + [{"grid": (g + o) % ng} for o in range(1, ng)]
 
     def win_tile(i):
-        rows = pl.ds(pl.multiple_of(i * s.tile, s.tile), s.tile)
+        rows = pl.ds(i * s.tile, s.tile)
         return pltpu.make_async_copy(win_hbm.at[rows], win_s.at[rows], local_sem.at[3 + i])
 
     get_lat = pltpu.make_async_copy(lat_hbm, lat_s, local_sem.at[0])
@@ -97,12 +97,12 @@
     get_target = pltpu.make_async_copy(target_hbm, target_ref, local_sem.at[2])
     get_area = pltpu.make_async_copy(area_hbm, area_ref, local_sem.at[3 + s.tiles])
     get_vw = pltpu.make_async_copy(vw_hbm, vw_ref, local_sem.at[4 + s.tiles])
+    get_area.start()
+    get_vw.start()
+    get_out.start()
     get_lat.start()
     for i in range(s.tiles):
         win_tile(i).start()
-    get_out.start()
-    get_area.start()
-    get_vw.start()
     get_target.start()
     barrier = pltpu.get_barrier_semaphore()
     for peer in ens_peers[1:] + grid_peers[1:]:
@@ -112,19 +112,6 @@
     wo32[...] = jnp.zeros_like(wo32)
     tgt_s[...] = jnp.zeros_like(tgt_s)
 
-    get_lat.wait()
-    span = s.tile // (2 * s.cols)
-
-    def forward(i, carry):
-        rows = pl.ds(pl.multiple_of(i * s.tile, s.tile), s.tile)
-        win_tile(i).wait()
-        v = dot_nn(win_s[rows, :], lat_s[...].reshape(s.lat, s.pts))
-        t = jnp.tanh(GELU_C * (v + GELU_K * v * v * v))
-        hid_s[pl.ds(i * span, span)] = (0.5 * v * (1.0 + t)).astype(BF16).reshape(span, 2, s.cols, s.pts)
-        slope_s[rows, :] = 0.5 * (1.0 + t) + 0.5 * v * (1.0 - t * t) * GELU_C * (1.0 + 3.0 * GELU_K * v * v)
-        return carry
-
-    lax.fori_loop(0, s.tiles, forward, 0)
     get_area.wait()
     get_vw.wait()
     arow = area_ref[...].reshape(1, s.pts)
@@ -133,6 +120,18 @@
     get_out.wait()
     wo32[0:s.nvars, :] = wout_ref[...].astype(F32)
     wo_s[...] = wo32[...].astype(BF16)
+
+    get_lat.wait()
+    span = s.tile // (2 * s.cols)
+
+    for i in range(s.tiles):
+        rows = pl.ds(i * s.tile, s.tile)
+        win_tile(i).wait()
+        v = dot_nn(win_s[rows, :], lat_s[...].reshape(s.lat, s.pts))
+        t = jnp.tanh(GELU_C * (v + GELU_K * v * v * v))
+        hid_s[pl.ds(i * span, span)] = (0.5 * v * (1.0 + t)).astype(BF16).reshape(span, 2, s.cols, s.pts)
+        pre_s[rows, :] = v
+        slope_s[rows, :] = t
     dec_s[...] = dot_nn(wo_s[...], hid_s[...].reshape(s.hid, s.pts)).reshape(n, s.vrow, s.pts)
     pl.semaphore_wait(barrier, n + ng - 2)
 
@@ -151,14 +150,10 @@
     mine = pl.ds(pl.multiple_of(me * s.vrow, s.vrow), s.vrow)
     weight = vcol_s[mine, 0:1] * arow
     target = tgt_s[mine, :]
-    turned = s.lat // 4
-
-    def turn(j):
-        at = pl.ds(j * turned, turned)
-        wint[at, :] = win_s[:, at].T
-
-    turn(0)
-    turn(1)
+    for i in range(s.tiles):
+        rows = pl.ds(i * s.tile, s.tile)
+        v, t = pre_s[rows, :], slope_s[rows, :]
+        slope_s[rows, :] = 0.5 * (1.0 + t) + 0.5 * v * (1.0 - t * t) * GELU_C * (1.0 + 3.0 * GELU_K * v * v)
     for copy in area_copies:
         copy.wait_recv()
     total = area_all[0]
@@ -198,8 +193,6 @@
     loss_e[0] = jnp.broadcast_to(part, (8, 128))
     loss_copies = [remote(loss_e.at[0], loss_e.at[r], ens_peers[r]) for r in range(1, n)]
 
-    turn(2)
-    turn(3)
     for copy in dout_copies:
         copy.wait_recv()
     dout_copy = remote(dout_s, doutp, twin)
@@ -276,12 +269,13 @@
             moves[k] = [start(acc.at[k, h], snd.at[k, h], rcv[0].at[k, h], orders[h], 0) for h in range(2)]
 
 
+    quarter = s.lat // 4
+
     def latent_part(j):
-        at = pl.ds(j * turned, turned)
-        glat_ref[0, at, :] = dot_nn(wint[at, :], dpre_s[...]).astype(BF16)
+        at = pl.ds(j * quarter, quarter)
+        glat_ref[0, at, :] = dot_tn(win_s[:, at], dpre_s[...]).astype(BF16)
 
     latent_part(0)
-    latent_part(1)
     zero = (0,) * nb
     out_moves = []
 
@@ -295,8 +289,7 @@
         return None
 
     out_copy = out_step(out_copy, 0)
-    latent_part(2)
-    latent_part(3)
+    latent_part(1)
     for copy in loss_copies:
         copy.wait_recv()
     here = loss_e[0]
@@ -305,7 +298,10 @@
     loss_g[0] = here
     loss_copies = [remote(loss_g.at[0], loss_g.at[o], grid_peers[o]) for o in range(1, ng)]
     ratio = float(1.0 / np.sqrt(np.float32(ng * s.pts) * np.float32(n)))
+    early = len(sent)
     for step in range(nz + nb - 1):
+        if step in (1, 2):
+            latent_part(step + 1)
         for stage in range(nb):
             k = step - stage
             if not 0 <= k < nz:
@@ -319,6 +315,9 @@
                 moves[k] = remote(zsnd.at[k], zrcv.at[k], {"grid": chip_at(k) * 2 + core})
         if step + 1 < nb:
             out_copy = out_step(out_copy, step + 1)
+        if step == 2:
+            for copy in sent[:early]:
+                copy.wait_send()
         if step == nz + nb - 3:
             block = acc_o[zero + (nz - 1,)]
             for k in range(nz - 1):
@@ -341,15 +340,20 @@
     for copy in gathers:
         copy.wait_recv()
     gout_ref[...] = gall[0:s.nvars, :]
-    for copy in sent:
+    for copy in sent[early:]:
         copy.wait_send()
 
 
-def hand_out(a, b, c, a_out, b_out, c_out, sem):
-    copies = [pltpu.make_async_copy(x, y, sem.at[i]) for i, (x, y) in enumerate(((a, a_out), (b, b_out), (c, c_out)))]
-    for copy in copies:
+def hand_out(*refs):
+    sources, targets, held, sems = refs[:3], refs[3:6], refs[6:9], refs[9]
+    reads = [pltpu.make_async_copy(x, y, sems.at[0, i]) for i, (x, y) in enumerate(zip(sources, held))]
+    writes = [pltpu.make_async_copy(x, y, sems.at[1, i]) for i, (x, y) in enumerate(zip(held, targets))]
+    for copy in reads:
         copy.start()
-    for copy in copies:
+    for read, write in zip(reads, writes):
+        read.wait()
+        write.start()
+    for copy in writes:
         copy.wait()
 
 
@@ -367,7 +371,6 @@
         pltpu.VMEM((nz, 2, cols, pts), BF16),
         pltpu.VMEM((nz, cols, pts), BF16),
         pltpu.VMEM((hid, lat), BF16),
-        pltpu.VMEM((lat, hid), BF16),
         pltpu.VMEM((nvars, hid), BF16),
         pltpu.VMEM((nvars, pts), F32),
         pltpu.VMEM((pts,), F32),
@@ -377,6 +380,7 @@
         pltpu.VMEM((hid, s.vpad), BF16),
         pltpu.VMEM((nz, 2, cols, pts), BF16),
         pltpu.VMEM((nz, cols, pts), BF16),
+        pltpu.VMEM((hid, pts), F32),
         pltpu.VMEM((hid, pts), F32),
         pltpu.VMEM((n, s.vrow, pts), F32),
         pltpu.VMEM((n, s.vrow, pts), F32),
@@ -429,9 +433,10 @@
     grad_lat, grad_in, grad_out = pl.pallas_call(
         hand_out,
         out_shape=tuple(jax.ShapeDtypeStruct(x.shape, x.dtype) for x in (grad_lat, grad_in, grad_out)),
-        in_specs=[vmem] * 3,
+        in_specs=[hbm] * 3,
         out_specs=(hbm,) * 3,
-        scratch_shapes=[pltpu.SemaphoreType.DMA((3,))],
+        scratch_shapes=[pltpu.VMEM(x.shape, x.dtype) for x in (grad_lat, grad_in, grad_out)]
+        + [pltpu.SemaphoreType.DMA((2, 3))],
         compiler_params=pltpu.CompilerParams(vmem_limit_bytes=VMEM_BYTES),
         name="hand_out",
     )(grad_lat, grad_in, grad_out)

time: 41.3 us -> 41.7 us (level)
    pallas_call x1, Pallas kernels: 36.7 us -> 37.1 us  [per_device(): pl.pallas_call(functools.partial(kernel, s), out_shape=(jax.ShapeDtypeStr...]
where the time goes in v4:
time: 41.7 us; the launch traced here: 41.5 us
  Pallas kernels  39.1 us (94%)
  between operations  2.44 us (6%)
    pallas_call x1, Pallas kernels, per_device(): pl.pallas_call(functools.partial(kernel, s), out_shape=(jax.ShapeDtypeStr...  37.1 us
    pallas_call x1, Pallas kernels, per_device(): pl.pallas_call(hand_out, out_shape=tuple((jax.ShapeDtypeStruct(x.shape, x...  1.93 us

profile of v4, /device:TPU:0, one launch (start us, length us, event | category | flops | bytes accessed | tf_op | source)
XLA Modules:
  0.0 41.5 jit_solution(12903736949587063674)
XLA Ops:
  0.6 37.1 %crps_backward.1 = (f32[1,1]{1,0:T(1,128)}, bf16[1,1024,256]{2,1,0:T(8,128)(2,1)}, f32[256,128]{1,0:T(8,128)}, f32[99,128]{1,0:T(8,128)}) custom-call(bf16[4,2,128,256]{3,2,1,0:T(8,128)(2,1)} %bitcast.2, bf16[1024,1024]{1,0:T(8,128)(2,1)} %win_hbm.1, bf16[99,1024]{1,0:T(8,128)(2,1)} %wout_hbm.1, f32[99,256]{1,0:T(8,128)} %target_hbm.1, f32[256]{0:T(256)} %area_hbm.1, ...), custom_call_target="tpu_custom_call" | custom-call | tf_op jit(solution)/shard_map/crps_backward/pallas_call | solution.py:417
  37.8 1.9 %hand_out.1 = (bf16[1,1024,256]{2,1,0:T(8,128)(2,1)}, f32[256,128]{1,0:T(8,128)}, f32[99,128]{1,0:T(8,128)}) custom-call(bf16[1,1024,256]{2,1,0:T(8,128)(2,1)} %get-tuple-element.12.refs_0_, f32[256,128]{1,0:T(8,128)} %get-tuple-element.13.refs_1_, f32[99,128]{1,0:T(8,128)} %get-tuple-element.14.refs_2_), custom_call_target="tpu_custom_call" | custom-call | tf_op jit(solution)/shard_map/hand_out/pallas_call | solution.py:433

commit v5 on v4

--- a/solution.py
+++ b/solution.py
@@ -14,6 +14,7 @@
 F32 = jnp.float32
 BF16 = jnp.bfloat16
 VMEM_BYTES = 62 * 1024 * 1024
+AHEAD = 2
 
 
 def dot_nn(a, b):
@@ -203,8 +204,10 @@
         dpre_s[rows, :] = (dot_nn(wot[rows, :], dout) * slope_s[rows, :]).astype(BF16)
         dpre_copies.append(remote(dpre_s.at[rows], dprep.at[rows], twin))
 
+    offsets = [nz // 2] + [o for o in range(nz - 1, 0, -1) if o != nz // 2] + [0]
+
     def chip_at(k):
-        return (chip + nz - 1 - k) % nz
+        return (chip + offsets[k]) % nz
 
     up, down = list(range(nb)), list(range(nb))[::-1]
 
@@ -246,6 +249,10 @@
 
     moves = [None] * nz
     orders = (up, down)
+
+    def first_stage(k):
+        moves[k] = [start(acc.at[k, h], snd.at[k, h], rcv[0].at[k, h], orders[h], 0) for h in range(2)]
+
     lat_copy.wait_recv()
     for first in range(0, nz, group):
         zs = [chip_at(k) for k in range(first, first + group)]
@@ -266,7 +273,8 @@
                     base = ens_peer(r) * s.rows_e + h * s.half
                     value = tmp[pl.ds(pl.multiple_of(base, s.half), s.half), lanes]
                     place(value, acc, snd, (k, h) + relative(r), r, orders[h])
-            moves[k] = [start(acc.at[k, h], snd.at[k, h], rcv[0].at[k, h], orders[h], 0) for h in range(2)]
+            if k < AHEAD:
+                first_stage(k)
 
 
     quarter = s.lat // 4
@@ -310,6 +318,8 @@
                 absorb(moves[k][h], acc.at[k, h], rcv[stage].at[k, h], order, stage)
                 if stage < nb - 1:
                     moves[k][h] = start(acc.at[k, h], snd.at[k, h], rcv[stage + 1].at[k, h], order, stage + 1)
+            if stage == 0 and k + AHEAD < nz:
+                first_stage(k + AHEAD)
             if stage == nb - 1 and k < nz - 1:
                 zsnd[k] = acc[(k, slice(None)) + zero].astype(BF16)
                 moves[k] = remote(zsnd.at[k], zrcv.at[k], {"grid": chip_at(k) * 2 + core})

time: 41.7 us -> 39.1 us (0.938)
  Pallas kernels: 39.1 us -> 36.5 us
    pallas_call x1, Pallas kernels: 37.1 us -> 34.6 us  [per_device(): pl.pallas_call(functools.partial(kernel, s), out_shape=(jax.ShapeDtypeStr...]
where the time goes in v5:
time: 39.1 us; the launch traced here: 38.9 us
  Pallas kernels  36.5 us (93%)
  between operations  2.44 us (6%)
    pallas_call x1, Pallas kernels, per_device(): pl.pallas_call(functools.partial(kernel, s), out_shape=(jax.ShapeDtypeStr...  34.6 us
    pallas_call x1, Pallas kernels, per_device(): pl.pallas_call(hand_out, out_shape=tuple((jax.ShapeDtypeStruct(x.shape, x...  1.93 us

profile of v5, /device:TPU:0, one launch (start us, length us, event | category | flops | bytes accessed | tf_op | source)
XLA Modules:
  0.0 38.9 jit_solution(15126018809753981953)
XLA Ops:
  0.6 34.6 %crps_backward.1 = (f32[1,1]{1,0:T(1,128)}, bf16[1,1024,256]{2,1,0:T(8,128)(2,1)}, f32[256,128]{1,0:T(8,128)}, f32[99,128]{1,0:T(8,128)}) custom-call(bf16[4,2,128,256]{3,2,1,0:T(8,128)(2,1)} %bitcast.2, bf16[1024,1024]{1,0:T(8,128)(2,1)} %win_hbm.1, bf16[99,1024]{1,0:T(8,128)(2,1)} %wout_hbm.1, f32[99,256]{1,0:T(8,128)} %target_hbm.1, f32[256]{0:T(256)} %area_hbm.1, ...), custom_call_target="tpu_custom_call" | custom-call | tf_op jit(solution)/shard_map/crps_backward/pallas_call | solution.py:427
  35.2 1.9 %hand_out.1 = (bf16[1,1024,256]{2,1,0:T(8,128)(2,1)}, f32[256,128]{1,0:T(8,128)}, f32[99,128]{1,0:T(8,128)}) custom-call(bf16[1,1024,256]{2,1,0:T(8,128)(2,1)} %get-tuple-element.12.refs_0_, f32[256,128]{1,0:T(8,128)} %get-tuple-element.13.refs_1_, f32[99,128]{1,0:T(8,128)} %get-tuple-element.14.refs_2_), custom_call_target="tpu_custom_call" | custom-call | tf_op jit(solution)/shard_map/hand_out/pallas_call | solution.py:443
